TPU v7x, 128 devices: a whole 4x4x4 slice. The times are simulated.
128 devices in a mesh: dp: 64 (over y, z, x), split: 2 (over core).
Axes of the slice: x: 4, y: 4, z: 4, core: 2. Of those that a mesh axis runs over, the one named last changes fastest.
Arguments:
- embeddings: bfloat16 [131072, 768], P(('dp', 'split')), may hold values from -6 to 6
- cluster: int32 [131072], P(('dp', 'split')), may hold values from 0 to 511, as said below
- rank: int32 [131072], P(('dp', 'split')), may hold values from 0 to 131071, each once
Outputs:
- max_cosine: float32 [131072], P(('dp', 'split'))
Inputs may be any that keep to these rules, and one draw needn't show every extreme that they name: cluster // 8 names the row's owner, an index of dp. The rows of one device name each owner at most 32 times, and in every draw one owner is named exactly 32 times by the rows of every device.
All inputs are finite; a program needn't handle non-finite values.
Results may differ from a plain program's by a relative error of at most 0.0014.
Values may be sent and summed in bfloat16 or wider, within the bound.
A program may use at most 64 MiB of HBM per device.

v0:
```python
import jax
import jax.numpy as jnp
from jax import lax
from jax.sharding import PartitionSpec as P

CL_DEV = 8


def swapped(block, axis, bit):
    count = lax.axis_size(axis)
    route = []
    for low in range(count):
        high = low | 1 << bit
        if high != low and high < count:
            route += [(low, high), (high, low)]
    return lax.ppermute(block, axis, route)


def tile_size():
    return 512


def masked_max(queries, query_cluster, query_rank, keys, key_cluster, key_rank):
    count = queries.shape[0]
    width = queries.shape[1]
    block = tile_size()
    blocks = count // block
    key_valid = key_cluster >= 0

    def one_block(pieces):
        part_q, part_c, part_r = pieces
        scores = lax.dot_general(
            part_q, keys, (((1,), (1,)), ((), ())), preferred_element_type=jnp.float32
        )
        allowed = (
            (part_c[:, None] == key_cluster[None, :])
            & (key_rank[None, :] < part_r[:, None])
            & key_valid[None, :]
        )
        return jnp.max(jnp.where(allowed, scores, jnp.float32(-1.0)), axis=1)

    stacked = (
        queries.reshape(blocks, block, width),
        query_cluster.reshape(blocks, block),
        query_rank.reshape(blocks, block),
    )
    return lax.map(one_block, stacked).reshape(count)


def shards(embeddings, cluster, rank):
    local_rows = embeddings.shape[0]
    values = embeddings.astype(jnp.float32)
    unit = (values * lax.rsqrt(jnp.sum(values * values, axis=1, keepdims=True) + 1e-06)).astype(
        jnp.bfloat16
    )
    groups = lax.axis_size("dp")
    capacity = 2 * local_rows // groups
    owner = cluster // CL_DEV
    hits = owner[:, None] == jnp.arange(groups, dtype=jnp.int32)[None, :]
    positions = jnp.arange(local_rows, dtype=jnp.int32)
    lower = (positions[None, :] <= positions[:, None]).astype(jnp.bfloat16)
    running = jnp.dot(lower, hits.astype(jnp.bfloat16), preferred_element_type=jnp.float32)
    place = jnp.sum(jnp.where(hits, running, 0.0), axis=1).astype(jnp.int32) - 1
    target = owner * capacity + place
    slots = groups * capacity
    selector = jnp.arange(slots, dtype=jnp.int32)[:, None] == target[None, :]
    send_rows = jnp.dot(
        selector.astype(jnp.bfloat16), unit, preferred_element_type=jnp.float32
    ).astype(jnp.bfloat16)
    send_cluster = jnp.max(jnp.where(selector, cluster[None, :], -1), axis=1)
    send_rank = jnp.max(jnp.where(selector, rank[None, :], 0), axis=1)
    query_rows, query_cluster, query_rank = (
        lax.all_to_all(send_rows, "dp", split_axis=0, concat_axis=0, tiled=True),
        lax.all_to_all(send_cluster, "dp", split_axis=0, concat_axis=0, tiled=True),
        lax.all_to_all(send_rank, "dp", split_axis=0, concat_axis=0, tiled=True),
    )
    far_rows, far_cluster, far_rank = swapped((query_rows, query_cluster, query_rank), "split", 0)
    key_rows = jnp.concatenate([query_rows, far_rows], axis=0)
    key_cluster = jnp.concatenate([query_cluster, far_cluster])
    key_rank = jnp.concatenate([query_rank, far_rank])
    best = masked_max(query_rows, query_cluster, query_rank, key_rows, key_cluster, key_rank)
    returned = lax.all_to_all(best, "dp", split_axis=0, concat_axis=0, tiled=True)
    return jnp.sum(jnp.where(selector, returned[:, None], jnp.float32(0.0)), axis=0)


def solution(mesh):
    in_specs = (P(("dp", "split"), None), P(("dp", "split")), P(("dp", "split")))
    out_specs = P(("dp", "split"))
    return jax.shard_map(shards, mesh=mesh, in_specs=in_specs, out_specs=out_specs, check_vma=False)
```

profile of v0, /device:TPU:0, one launch (start us, length us, event | category | flops | bytes accessed | tf_op | source)
XLA Modules:
  0.0 147.9 jit_solution(1473292172949617573)
XLA Ops:
  0.0 0.7 add_select_fusion
  0.7 0.6 fusion.12
  1.3 0.7 add_add_fusion
  2.0 1.8 %fusion.7 = f32[1024]{0:T(1024)S(1)} fusion(bf16[1024,768]{1,0:T(8,128)(2,1)} %param.5), kind=kLoop, calls=%fused_computation.18 | loop fusion | flops 2358272 | bytes 1576960 | tf_op jit(solution)/shard_map/reduce_sum | solution.py:53
  3.8 5.7 %fusion.6 = bf16[2048,768]{1,0:T(8,128)(2,1)S(1)} fusion(s32[1024]{0:T(1024)S(1)} %add_add_fusion, bf16[1024,768]{1,0:T(8,128)(2,1)} %param.5, f32[1024]{0:T(1024)S(1)} %add_rsqrt_fusion), kind=kOutput, calls=%fused_computation.17 | convolution fusion | flops 3227254784 | bytes 4726784 | tf_op jit(solution)/shard_map/dot_general | solution.py:67
  9.5 0.0 copy-start
  9.5 0.0 copy-start.1
  9.5 52.7 %all_to_all.45 = bf16[64,32,768]{2,1,0:T(8,128)(2,1)S(1)} all-to-all(bf16[64,32,768]{2,1,0:T(8,128)(2,1)S(1)} %bitcast.31), channel_id=1, replica_groups=mesh['dp'=64,'split'=2] {'dp'}, dimensions={0} | all-to-all | bytes 6291456 | tf_op jit(solution)/shard_map/all_to_all | solution.py:73
  62.2 0.0 collective-permute-start.2
  62.2 0.0 copy-done
  62.2 0.0 copy-done.1
  62.2 2.9 %select_reduce_fusion.2 = (s32[2048]{0:T(1024)S(1)}, s32[2048]{0:T(1024)S(1)}) fusion(s32[1024]{0:T(1024)S(1)} %copy-done.1, s32[1024]{0:T(1024)S(1)} %add_add_fusion, s32[1024]{0:T(1024)S(1)} %copy-done), kind=kLoop, calls=%fused_computation.7 | loop fusion | flops 10481664 | bytes 28672 | tf_op jit(solution)/shard_map/reduce_max | solution.py:71
  65.1 0.7 all_to_all.30
  65.8 5.2 %all-to-all-start = ((s32[64,32,1]{1,2,0:T(1,128)}), s32[64,32,1]{1,2,0:T(1,128)S(1)}, u32[]{:S(2)}, u32[]{:S(2)}) async-start(s32[64,32,1]{1,2,0:T(1,128)} %bitcast.4), calls=%async_computation | async-start | bytes 65536 | tf_op jit(solution)/shard_map/all_to_all | solution.py:74
  71.0 0.7 all_to_all.33
  71.7 8.9 %all-to-all-done = s32[64,32,1]{1,2,0:T(1,128)S(1)} async-done(((s32[64,32,1]{1,2,0:T(1,128)}), s32[64,32,1]{1,2,0:T(1,128)S(1)}, u32[]{:S(2)}, u32[]{:S(2)}) %all-to-all-start) | async-done | bytes 8224 | tf_op jit(solution)/shard_map/all_to_all | solution.py:74
  80.5 5.0 %all-to-all-start.1 = ((s32[64,32,1]{1,2,0:T(1,128)}), s32[64,32,1]{1,2,0:T(1,128)S(1)}, u32[]{:S(2)}, u32[]{:S(2)}) async-start(s32[64,32,1]{1,2,0:T(1,128)} %bitcast.5), calls=%async_computation.1 | async-start | bytes 65536 | tf_op jit(solution)/shard_map/all_to_all | solution.py:75
  85.5 0.1 all_to_all.32
  85.6 0.0 collective-permute-start
  85.6 0.5 broadcast.44
  86.1 0.7 reduce.13
  86.9 0.1 reshape.41
  86.9 8.0 %all-to-all-done.1 = s32[64,32,1]{1,2,0:T(1,128)S(1)} async-done(((s32[64,32,1]{1,2,0:T(1,128)}), s32[64,32,1]{1,2,0:T(1,128)S(1)}, u32[]{:S(2)}, u32[]{:S(2)}) %all-to-all-start.1) | async-done | bytes 8224 | tf_op jit(solution)/shard_map/all_to_all | solution.py:75
  95.0 0.7 reduce.14
  95.7 0.1 all_to_all.35
  95.8 0.2 collective-permute-start.1
  96.0 0.1 reshape.42
  96.1 0.0 collective-permute-done
  96.1 1.1 collective-permute-done.1
  97.2 0.0 collective-permute-done.2
  97.2 5.0 %pad_maximum_fusion = bf16[4096,768]{1,0:T(8,128)(2,1)} fusion(bf16[2048,768]{1,0:T(8,128)(2,1)} %collective-permute-done.2, bf16[2048,768]{1,0:T(8,128)(2,1)S(1)} %bitcast.29), kind=kLoop, calls=%fused_computation.11 | loop fusion | flops 12582912 | bytes 12582912 | tf_op jit(solution)/shard_map/concatenate | solution.py:78
  102.1 28.5 %while.10 = (s32[]{:T(128)}, f32[4,512]{1,0:T(4,128)S(1)}, s32[4,512]{1,0:T(4,128)S(1)}, s32[4096]{0:T(1024)S(1)}, s32[4096]{0:T(1024)S(1)}, /*index=5*/s32[4,51...) while((s32[]{:T(128)}, f32[4,512]{1,0:T(4,128)S(1)}, ...), condition=%wide.region_6.7_spmd, body=%wide.region_4.6_spmd.sunk | while | flops 3233807872 | bytes 7133313 | solution.py:47
  102.2 7.0 %select_reduce_fusion.5 = f32[512]{0:T(512)S(1)} fusion(bf16[4096,768]{1,0:T(8,128)(2,1)} %get-tuple-element.164, s32[4096]{0:T(1024)S(1)} %get-tuple-element.160, s32[4096]{0:T(1024)S(1)} %get-tuple-element.159, s32[512]{0:T(512)S(1)} %bitcast.35, s32[512]{0:T(512)S(1)} %bitcast.36, pred[4096]{0:T(1024)(128)(4,1)S(1)} %get-tuple-element.162, ...), kind=kOutput, calls=%fused_computation.clone.1 | convolution fusion | flops 3233807872 | bytes 7120900 | tf_op jit(solution)/shard_map/while/body/eval_jaxpr/dot_general | solution.py:32
  109.3 7.0 %select_reduce_fusion.5 = f32[512]{0:T(512)S(1)} fusion(bf16[4096,768]{1,0:T(8,128)(2,1)} %get-tuple-element.164, s32[4096]{0:T(1024)S(1)} %get-tuple-element.160, s32[4096]{0:T(1024)S(1)} %get-tuple-element.159, s32[512]{0:T(512)S(1)} %bitcast.35, s32[512]{0:T(512)S(1)} %bitcast.36, pred[4096]{0:T(1024)(128)(4,1)S(1)} %get-tuple-element.162, ...), kind=kOutput, calls=%fused_computation.clone.1 | convolution fusion | flops 3233807872 | bytes 7120900 | tf_op jit(solution)/shard_map/while/body/eval_jaxpr/dot_general | solution.py:32
  116.4 7.0 %select_reduce_fusion.5 = f32[512]{0:T(512)S(1)} fusion(bf16[4096,768]{1,0:T(8,128)(2,1)} %get-tuple-element.164, s32[4096]{0:T(1024)S(1)} %get-tuple-element.160, s32[4096]{0:T(1024)S(1)} %get-tuple-element.159, s32[512]{0:T(512)S(1)} %bitcast.35, s32[512]{0:T(512)S(1)} %bitcast.36, pred[4096]{0:T(1024)(128)(4,1)S(1)} %get-tuple-element.162, ...), kind=kOutput, calls=%fused_computation.clone.1 | convolution fusion | flops 3233807872 | bytes 7120900 | tf_op jit(solution)/shard_map/while/body/eval_jaxpr/dot_general | solution.py:32
  123.5 7.0 %select_reduce_fusion.5 = f32[512]{0:T(512)S(1)} fusion(bf16[4096,768]{1,0:T(8,128)(2,1)} %get-tuple-element.164, s32[4096]{0:T(1024)S(1)} %get-tuple-element.160, s32[4096]{0:T(1024)S(1)} %get-tuple-element.159, s32[512]{0:T(512)S(1)} %bitcast.35, s32[512]{0:T(512)S(1)} %bitcast.36, pred[4096]{0:T(1024)(128)(4,1)S(1)} %get-tuple-element.162, ...), kind=kOutput, calls=%fused_computation.clone.1 | convolution fusion | flops 3233807872 | bytes 7120900 | tf_op jit(solution)/shard_map/while/body/eval_jaxpr/dot_general | solution.py:32
  130.6 0.1 all_to_all.39
  130.7 14.3 %all_to_all.46 = f32[64,32,1]{1,2,0:T(1,128)S(1)} all-to-all(f32[64,32,1]{1,2,0:T(1,128)S(1)} %bitcast.34), channel_id=1, replica_groups=mesh['dp'=64,'split'=2] {'dp'}, dimensions={0} | all-to-all | bytes 16384 | tf_op jit(solution)/shard_map/all_to_all | solution.py:82
  145.1 0.5 broadcast.46
  145.6 0.7 reduce.15
  146.3 0.1 broadcast_in_dim.70
  146.4 1.6 %select_reduce_fusion.1 = f32[1024]{0:T(1024)} fusion(f32[2048]{0:T(1024)S(1)} %broadcast_in_dim.70, s32[1024]{0:T(1024)S(1)} %add_add_fusion), kind=kLoop, calls=%fused_computation.6 | loop fusion | flops 6290432 | bytes 16384 | tf_op jit(solution)/shard_map/reduce_sum | solution.py:83
  (14 shorter events, 0.2 us)
Async XLA Ops:
  9.5 52.7 %copy-start = (s32[1024]{0:T(1024)S(1)}, s32[1024]{0:T(1024)}, u32[]{:S(2)}) copy-start(s32[1024]{0:T(1024)} %param.6) | copy-start | bytes 12292
  9.5 52.7 %copy-start.1 = (s32[1024]{0:T(1024)S(1)}, s32[1024]{0:T(1024)}, u32[]{:S(2)}) copy-start(s32[1024]{0:T(1024)} %param.7) | copy-start | bytes 12292
  62.2 35.0 %collective-permute-start.2 = (bf16[2048,768]{1,0:T(8,128)(2,1)S(1)}, bf16[2048,768]{1,0:T(8,128)(2,1)}, u32[]{:S(2)}, u32[]{:S(2)}) collective-permute-start(bf16[2048,768]{1,0:T(8,128)(2,1)S(1)} %bitcast.28), channel_id=1, source_target_pairs={{0,1},{1,0},{2,3},{3,2},{4,5},{5,4},{6,7},{7,6},{8,9},{9,8},{10,11... | collective-permute-start | bytes 9437192 | tf_op jit(solution)/shard_map/ppermute | solution.py:16
  65.8 14.7 %all-to-all-start = ((s32[64,32,1]{1,2,0:T(1,128)}), s32[64,32,1]{1,2,0:T(1,128)S(1)}, u32[]{:S(2)}, u32[]{:S(2)}) async-start(s32[64,32,1]{1,2,0:T(1,128)} %bitcast.4), calls=%async_computation | async-start | bytes 65536 | tf_op jit(solution)/shard_map/all_to_all | solution.py:74
  80.5 14.5 %all-to-all-start.1 = ((s32[64,32,1]{1,2,0:T(1,128)}), s32[64,32,1]{1,2,0:T(1,128)S(1)}, u32[]{:S(2)}, u32[]{:S(2)}) async-start(s32[64,32,1]{1,2,0:T(1,128)} %bitcast.5), calls=%async_computation.1 | async-start | bytes 65536 | tf_op jit(solution)/shard_map/all_to_all | solution.py:75
  85.6 10.5 %collective-permute-start = (s32[2048]{0:T(1024)S(1)}, s32[2048]{0:T(1024)S(1)}, u32[]{:S(2)}, u32[]{:S(2)}) collective-permute-start(s32[2048]{0:T(1024)S(1)} %all_to_all.32), channel_id=1, source_target_pairs={{0,1},{1,0},{2,3},{3,2},{4,5},{5,4},{6,7},{7,6},{8,9},{9,8},{10,11... | collective-permute-start | bytes 24584 | tf_op jit(solution)/shard_map/ppermute | solution.py:16
  95.8 1.4 collective-permute-start.1
where the time goes:
time: 149 us; the launch traced here: 148 us
  blocking collectives  67.1 us (45%)
  matrix products  34.4 us (23%)
  waiting for transfers between devices  18 us (12%)
  other arithmetic  14.8 us (10%)
  starting transfers between devices  10.3 us (7%)
  local copies, waits for them, and re-layouts  3.11 us (2%)
    all_to_all x1, blocking collectives, shards(): lax.all_to_all(send_rows, 'dp', split_axis=0, concat_axis=0, tiled=True)  52.7 us
    dot_general x4, matrix products, one_block(): lax.dot_general(part_q, keys, (((1,), (1,)), ((), ())), preferred_element...  28.2 us
    all_to_all x1, blocking collectives, shards(): lax.all_to_all(best, 'dp', split_axis=0, concat_axis=0, tiled=True)  14.3 us
    all_to_all x1, waiting for transfers between devices, shards(): lax.all_to_all(send_cluster, 'dp', split_axis=0, concat_axis=0, tiled=True)  8.87 us
    all_to_all x1, waiting for transfers between devices, shards(): lax.all_to_all(send_rank, 'dp', split_axis=0, concat_axis=0, tiled=True)  8.05 us
    dot_general x1, matrix products, shards(): jnp.dot(selector.astype(jnp.bfloat16), unit, preferred_element_type=jnp.f...  5.67 us
    all_to_all x1, starting transfers between devices, shards(): lax.all_to_all(send_cluster, 'dp', split_axis=0, concat_axis=0, tiled=True)  5.15 us
    concatenate x1, other arithmetic, shards(): key_rows = jnp.concatenate([query_rows, far_rows], axis=0)  4.96 us
  transfers between devices with their start and end apart: 5, of which 3 were waited for; matrix products, arithmetic and copies ran while one was open for 3% of the time, Pallas kernels for 0%

commit v1 on v0

v1 whole, which is shorter than its diff:
```python
import jax
import jax.numpy as jnp
from jax import lax
from jax.experimental import pallas as pl
from jax.experimental.pallas import tpu as pltpu
from jax.sharding import PartitionSpec as P

MESH = pl.DeviceIdType.MESH
OWNERS = 64
CAP = 32
ROWS = 1024
D = 768
RANKS = 131072
GROUP = 8
GROUPS = OWNERS // GROUP
WIDE = GROUP * CAP
EMPTY = 16777216.0


def link_load(step):
    load = []
    for part in step:
        load += [1 if part in (1, 2) else 0, 1 if part in (3, 2) else 0]
    return load


def balanced_order():
    left = [
        (index // 16, index // 4 % 4, index % 4)
        for index in sorted(range(1, OWNERS), key=lambda index: index * 37 % 64)
    ]
    total = [0] * 6
    order = [(0, 0, 0)]

    def score(step):
        sums = [a + b for a, b in zip(total, link_load(step))]
        return max(sums) - min(sums), -sum(min(part, 4 - part) for part in step)

    while left:
        best = min(left, key=score)
        left.remove(best)
        order.append(best)
        total = [a + b for a, b in zip(total, link_load(best))]
    return order


ORDER = balanced_order()


def nt_dot(a, b):
    return lax.dot_general(a, b, (((1,), (1,)), ((), ())), preferred_element_type=jnp.float32)


def kernel(
    emb_hbm, cluster_hbm, rank_hbm, out_ref,
    emb, cluster, rank, unit, hits, place, sel, picks,
    send_rows, own_rows, far_rows, send_codes, own_codes, far_codes,
    own_keys, far_keys, limits, best, send_back, got_back,
    load_sem, row_send, row_recv, code_send, code_recv, far_send, far_recv, back_send, back_recv,
):
    me = lax.axis_index("dp")
    core = lax.axis_index("split")
    my, mz, mx = me // 16, me // 4 % 4, me % 4

    def peer(step, sign):
        y = (my + sign * step[0] + 4) % 4
        z = (mz + sign * step[1] + 4) % 4
        x = (mx + sign * step[2] + 4) % 4
        return (y * 16 + z * 4 + x, core)

    sibling = (me, 1 - core)

    loads = [
        pltpu.make_async_copy(source, target, load_sem.at[index])
        for index, (source, target) in enumerate(
            ((cluster_hbm, cluster), (rank_hbm, rank), (emb_hbm, emb))
        )
    ]
    for load in loads:
        load.start()
    barrier = pltpu.get_barrier_semaphore()
    for step in ORDER[1:]:
        pl.semaphore_signal(barrier, inc=1, device_id=peer(step, 1), device_id_type=MESH)
    pl.semaphore_signal(barrier, inc=1, device_id=sibling, device_id_type=MESH)

    loads[0].wait()
    loads[1].wait()
    slot = lax.broadcasted_iota(jnp.int32, (OWNERS, 128), 0)
    route = jnp.zeros((OWNERS, 128), jnp.int32)
    for index, step in enumerate(ORDER):
        route = jnp.where(slot == index, step[0] * 16 + step[1] * 4 + step[2], route)
    digits = []
    for tile in range(8):
        ids = cluster[tile : tile + 1, :]
        owner = ids // 8
        step_y = (owner // 16 - my + 4) % 4
        step_z = (owner // 4 % 4 - mz + 4) % 4
        step_x = (owner % 4 - mx + 4) % 4
        code = step_y * 16 + step_z * 4 + step_x
        hit = jnp.where(route == code, 1.0, 0.0)
        hits[:, tile * 128 : (tile + 1) * 128] = hit.astype(jnp.bfloat16)
        code = ids % 8 * RANKS + rank[tile : tile + 1, :] + 1
        digits.append((code % 256, code // 256 % 256, code // 65536))
    lower = lax.broadcasted_iota(jnp.int32, (256, 256), 0)
    upper = lax.broadcasted_iota(jnp.int32, (256, 256), 1)
    before = jnp.where(lower <= upper, 1.0, 0.0).astype(jnp.bfloat16)
    carry = jnp.zeros((OWNERS, 1), jnp.float32)
    for part in range(4):
        cols = slice(part * 256, (part + 1) * 256)
        count = jnp.dot(hits[:, cols], before, preferred_element_type=jnp.float32) + carry
        carry = count[:, 255:256]
        place[:, cols] = jnp.where(hits[:, cols].astype(jnp.float32) > 0.5, count, 0.0)
    digit = jnp.concatenate(
        [jnp.concatenate([piece[row] for piece in digits], axis=1) for row in range(3)]
        + [jnp.zeros((5, ROWS), jnp.int32)],
        axis=0,
    )
    digit = digit.astype(jnp.float32).astype(jnp.bfloat16)

    loads[2].wait()

    def normalise(index, _):
        rows = pl.ds(pl.multiple_of(index * 128, 128), 128)
        values = emb[rows, :].astype(jnp.float32)
        total = jnp.sum(values * values, axis=1, keepdims=True)
        unit[rows, :] = (values * lax.rsqrt(total + 1e-06)).astype(jnp.bfloat16)
        return 0

    lax.fori_loop(0, 8, normalise, 0)

    spot = lax.broadcasted_iota(jnp.int32, (CAP, ROWS), 0).astype(jnp.float32) + 1.0
    row_copies, code_copies = [], []
    for group in range(GROUPS):
        for index in range(GROUP):
            line = place[group * GROUP + index : group * GROUP + index + 1, :]
            chosen = jnp.where(jnp.broadcast_to(line, (CAP, ROWS)) == spot, 1.0, 0.0)
            sel[index * CAP : (index + 1) * CAP, :] = chosen.astype(jnp.bfloat16)
        picked = jnp.dot(sel[...], unit[...], preferred_element_type=jnp.float32)
        picked = picked.astype(jnp.bfloat16).reshape(GROUP, CAP, D)
        send_rows[group * GROUP : (group + 1) * GROUP] = picked
        parts = nt_dot(digit, sel[...])
        codes = parts[0:1] + parts[1:2] * 256.0 + parts[2:3] * 65536.0
        for index in range(GROUP):
            half = index // 4 * 128
            send_codes[group * GROUP + index] = codes[:, half : half + 128]
        if group == 0:
            own_rows[0] = picked[0]
            own_codes[0] = codes[:, 0:128]
            pl.semaphore_wait(barrier, OWNERS)
        for index in range(max(1, group * GROUP), (group + 1) * GROUP):
            target = peer(ORDER[index], 1)
            copy = pltpu.make_async_remote_copy(
                src_ref=send_codes.at[index], dst_ref=own_codes.at[index],
                send_sem=code_send, recv_sem=code_recv,
                device_id=target, device_id_type=MESH,
            )
            copy.start()
            copy = pltpu.make_async_remote_copy(
                src_ref=send_rows.at[index], dst_ref=own_rows.at[index],
                send_sem=row_send, recv_sem=row_recv.at[group],
                device_id=target, device_id_type=MESH,
            )
            copy.start()

    turn = lax.broadcasted_iota(jnp.int32, (OWNERS, ROWS), 0) % 4 * CAP
    where = jnp.where(place[...] > 0.5, place[...] - 1.0 + turn.astype(jnp.float32), 0.0)
    where = jnp.sum(where, axis=0, keepdims=True)
    lane = lax.broadcasted_iota(jnp.int32, (128, ROWS), 0).astype(jnp.float32)
    picks[...] = jnp.where(lane == where, 1.0, 0.0).astype(jnp.bfloat16)

    def spread(codes, keys, is_own):
        block = codes[...].reshape(OWNERS // 4, 4, 1, 128)
        part = lax.broadcasted_iota(jnp.int32, block.shape, 1)
        at = lax.broadcasted_iota(jnp.int32, block.shape, 3) // CAP
        line = jnp.sum(jnp.where(part == at, block, 0.0), axis=1)
        if is_own:
            limits[0] = line
            limits[1] = jnp.floor((line - 1.0) * (1.0 / RANKS)) * float(RANKS) + 1.0
        line = jnp.where(line == 0.0, EMPTY, line)
        for index in range(OWNERS // 4):
            square = jnp.broadcast_to(line[index], (128, 128))
            keys[index * 128 : (index + 1) * 128, :] = square.T

    pltpu.make_async_copy(own_codes.at[1:], own_codes.at[1:], code_recv).wait()
    code_hop = pltpu.make_async_remote_copy(
        src_ref=own_codes, dst_ref=far_codes,
        send_sem=far_send.at[GROUPS], recv_sem=far_recv.at[GROUPS],
        device_id=sibling, device_id_type=MESH,
    )
    code_hop.start()
    spread(own_codes, own_keys, True)
    best[...] = jnp.full(best.shape, -1.0, jnp.float32)

    def compare(query, blocks):
        at = pl.multiple_of(query * GROUP, GROUP)
        rows = own_rows[pl.ds(at, GROUP)].reshape(WIDE, D)
        high = limits[0, pl.ds(query * 2, 2)]
        low = limits[1, pl.ds(query * 2, 2)]
        tops = [best[query, :, half * 128 : (half + 1) * 128] for half in range(2)]
        for data, keys, block in blocks:
            key_at = pl.multiple_of(block * GROUP, GROUP)
            scores = nt_dot(data[pl.ds(key_at, GROUP)].reshape(WIDE, D), rows)
            code = keys[pl.ds(pl.multiple_of(block * WIDE, WIDE), WIDE), :]
            for half in range(2):
                allowed = (code < high[half]) & (code >= low[half])
                part = scores[:, half * 128 : (half + 1) * 128]
                part = jnp.where(allowed, part, -1.0).reshape(WIDE // 8, 8, 128)
                tops[half] = jnp.maximum(tops[half], jnp.max(part, axis=0))
        for half in range(2):
            best[query, :, half * 128 : (half + 1) * 128] = tops[half]

    hops = []
    for step in range(GROUPS + 1):
        if step < GROUPS:
            here = own_rows.at[max(1, step * GROUP) : (step + 1) * GROUP]
            pltpu.make_async_copy(here, here, row_recv.at[step]).wait()
            block = pl.ds(step * GROUP, GROUP)
            hop = pltpu.make_async_remote_copy(
                src_ref=own_rows.at[block], dst_ref=far_rows.at[block],
                send_sem=far_send.at[step], recv_sem=far_recv.at[step],
                device_id=sibling, device_id_type=MESH,
            )
            hop.start()
            hops.append(hop)
        fresh = []
        if step < GROUPS:
            fresh.append((own_rows, own_keys, step))
        if step == 0:
            code_hop.wait_recv()
            spread(far_codes, far_keys, False)
        else:
            hops[step - 1].wait_recv()
            fresh.append((far_rows, far_keys, step - 1))

        def old_queries(query, _, fresh=fresh):
            compare(query, fresh)
            return 0

        if step < GROUPS:
            lax.fori_loop(0, step, old_queries, 0)

            def old_keys(block, _, step=step):
                compare(step, [(own_rows, own_keys, block), (far_rows, far_keys, block)])
                return 0

            lax.fori_loop(0, step, old_keys, 0)
            compare(step, [(own_rows, own_keys, step)])
        else:
            for query in range(GROUPS):
                compare(query, fresh)
                for half in range(2):
                    top = jnp.max(best[query, :, half * 128 : (half + 1) * 128], axis=0, keepdims=True)
                    send_back[query * 2 + half] = top
                for index in range(query * GROUP, (query + 1) * GROUP):
                    if index == 0:
                        got_back[0] = send_back[0]
                        continue
                    copy = pltpu.make_async_remote_copy(
                        src_ref=send_back.at[index // 4], dst_ref=got_back.at[index],
                        send_sem=back_send, recv_sem=back_recv,
                        device_id=peer(ORDER[index], -1), device_id_type=MESH,
                    )
                    copy.start()

    pltpu.make_async_copy(got_back.at[1:], got_back.at[1:], back_recv).wait()
    back = got_back[...].reshape(OWNERS, 128)
    first = back.astype(jnp.bfloat16)
    rest = back - first.astype(jnp.float32)
    second = rest.astype(jnp.bfloat16)
    third = (rest - second.astype(jnp.float32)).astype(jnp.bfloat16)
    moved = [
        jnp.dot(piece, picks[...], preferred_element_type=jnp.float32)
        for piece in (first, second, third)
    ]
    moved = moved[0] + moved[1] + moved[2]
    result = jnp.sum(jnp.where(place[...] > 0.5, moved, 0.0), axis=0, keepdims=True)
    for tile in range(8):
        out_ref[tile : tile + 1, :] = result[:, tile * 128 : (tile + 1) * 128]

    pltpu.make_async_copy(send_rows.at[1:], send_rows.at[1:], row_send).wait()
    pltpu.make_async_copy(send_codes.at[1:], send_codes.at[1:], code_send).wait()
    pltpu.make_async_copy(got_back.at[1:], got_back.at[1:], back_send).wait()
    code_hop.wait_send()
    for hop in hops:
        hop.wait_send()


def shards(embeddings, cluster, rank):
    rows = (OWNERS, CAP, D)
    codes = (OWNERS, 1, 128)
    f32, bf16 = jnp.float32, jnp.bfloat16
    dma = pltpu.SemaphoreType.DMA
    result = pl.pallas_call(
        kernel,
        out_shape=jax.ShapeDtypeStruct((8, 128), f32),
        in_specs=[pl.BlockSpec(memory_space=pltpu.HBM)] * 3,
        out_specs=pl.BlockSpec(memory_space=pltpu.VMEM),
        scratch_shapes=[
            pltpu.VMEM((ROWS, D), bf16),
            pltpu.VMEM((8, 128), jnp.int32),
            pltpu.VMEM((8, 128), jnp.int32),
            pltpu.VMEM((ROWS, D), bf16),
            pltpu.VMEM((OWNERS, ROWS), bf16),
            pltpu.VMEM((OWNERS, ROWS), f32),
            pltpu.VMEM((WIDE, ROWS), bf16),
            pltpu.VMEM((128, ROWS), bf16),
            pltpu.VMEM(rows, bf16),
            pltpu.VMEM(rows, bf16),
            pltpu.VMEM(rows, bf16),
            pltpu.VMEM(codes, f32),
            pltpu.VMEM(codes, f32),
            pltpu.VMEM(codes, f32),
            pltpu.VMEM((OWNERS * CAP, 128), f32),
            pltpu.VMEM((OWNERS * CAP, 128), f32),
            pltpu.VMEM((2, OWNERS // 4, 1, 128), f32),
            pltpu.VMEM((GROUPS, 8, WIDE), f32),
            pltpu.VMEM((OWNERS // 4, 1, 128), f32),
            pltpu.VMEM(codes, f32),
            dma((3,)),
            dma,
            dma((GROUPS,)),
            dma,
            dma,
            dma((GROUPS + 1,)),
            dma((GROUPS + 1,)),
            dma,
            dma,
        ],
        compiler_params=pltpu.CompilerParams(
            collective_id=0, has_side_effects=True, vmem_limit_bytes=40 * 2**20
        ),
        cost_estimate=pl.CostEstimate(
            flops=2 * D * 2048 * (4096 + 1024), bytes_accessed=2 * ROWS * D, transcendentals=ROWS
        ),
        name="dedup",
    )(embeddings, cluster.reshape(8, 128), rank.reshape(8, 128))
    return result.reshape(ROWS)


def solution(mesh):
    in_specs = (P(("dp", "split"), None), P(("dp", "split")), P(("dp", "split")))
    out_specs = P(("dp", "split"))
    return jax.shard_map(shards, mesh=mesh, in_specs=in_specs, out_specs=out_specs, check_vma=False)
```

time: 149 us -> 90.5 us (0.61)
  Pallas kernels: 0 us -> 86.8 us
  blocking collectives: 67.1 us -> 0 us
  matrix products: 34.4 us -> 0 us
  waiting for transfers between devices: 18 us -> 0 us
  other arithmetic: 14.8 us -> 0 us
  starting transfers between devices: 10.3 us -> 0 us
    pallas_call x0 -> x1, Pallas kernels: none -> 86.8 us  [shards(): pl.pallas_call(kernel, out_shape=jax.ShapeDtypeStruct((8, 128), f32), in_...]
    all_to_all x2 -> x0, blocking collectives: 67.1 us -> none  [the longest x1 52.7 us: shards(): lax.all_to_all(send_rows, 'dp', split_axis=0, concat_axis=0, tiled=True)]
    dot_general x6 -> x0, matrix products: 34.4 us -> none  [the longest x4 28.2 us: one_block(): lax.dot_general(part_q, keys, (((1,), (1,)), ((), ())), preferred_element...]
    all_to_all x2 -> x0, waiting for transfers between devices: 16.9 us -> none  [the longest x1 8.87 us: shards(): lax.all_to_all(send_cluster, 'dp', split_axis=0, concat_axis=0, tiled=True)]
    all_to_all x2 -> x0, starting transfers between devices: 10.1 us -> none  [the longest x1 5.15 us: shards(): lax.all_to_all(send_cluster, 'dp', split_axis=0, concat_axis=0, tiled=True)]
    concatenate x2 -> x0, other arithmetic: 4.96 us -> none  [the longest x1 4.96 us: shards(): key_rows = jnp.concatenate([query_rows, far_rows], axis=0)]
    unnamed x5 -> x7, local copies, waits for them, and re-layouts: 0.02 us -> 3.38 us
    reduce_sum x2 -> x0, other arithmetic: 3.34 us -> none  [the longest x1 1.78 us: shards(): jnp.sum(values * values, axis=1, keepdims=True) + 1e-06]
  transfers between devices with their start and end apart: 5 -> 0, of which waited for: 3 -> 0; matrix products, arithmetic and copies ran while one was open for 3% -> 0% of each run, Pallas kernels for 0% -> 0%
where the time goes in v1:
time: 90.5 us; the launch traced here: 90.2 us
  Pallas kernels  86.8 us (96%)
  local copies, waits for them, and re-layouts  3.38 us (4%)
    pallas_call x1, Pallas kernels, shards(): pl.pallas_call(kernel, out_shape=jax.ShapeDtypeStruct((8, 128), f32), in_...  86.8 us
    unnamed x7, local copies, waits for them, and re-layouts  3.38 us

profile of v1, /device:TPU:0, one launch (start us, length us, event | category | flops | bytes accessed | tf_op | source)
XLA Modules:
  0.0 90.2 jit_solution(2744765142787018752)
XLA Ops:
  0.0 0.0 copy-start
  0.0 1.4 %copy-done = bf16[1024,768]{1,0:T(8,128)(2,1)S(1)} copy-done((bf16[1024,768]{1,0:T(8,128)(2,1)S(1)}, bf16[1024,768]{1,0:T(8,128)(2,1)}, u32[]{:S(2)}) %copy-start) | copy-done | bytes 1572888
  1.4 0.0 copy-start.1
  1.4 0.7 copy-done.1
  2.1 0.0 copy-start.2
  2.1 0.7 copy-done.2
  2.8 86.8 %dedup.1 = f32[8,128]{1,0:T(8,128)S(1)} custom-call(bf16[1024,768]{1,0:T(8,128)(2,1)S(1)} %copy-done, s32[8,128]{1,0:T(8,128)S(1)} %bitcast.4, s32[8,128]{1,0:T(8,128)S(1)} %bitcast.5), custom_call_target="tpu_custom_call" | custom-call | flops 16106127360 | bytes 1572864 | tf_op jit(solution)/shard_map/dedup/pallas_call | solution.py:293
  89.6 0.6 copy.5
Async XLA Ops:
  0.0 1.4 %copy-start = (bf16[1024,768]{1,0:T(8,128)(2,1)S(1)}, bf16[1024,768]{1,0:T(8,128)(2,1)}, u32[]{:S(2)}) copy-start(bf16[1024,768]{1,0:T(8,128)(2,1)} %emb_hbm.1) | copy-start | bytes 4718596
  1.4 0.7 copy-start.1
  2.1 0.7 copy-start.2

commit v2 on v1

--- a/solution.py
+++ b/solution.py
@@ -15,6 +15,7 @@
 GROUPS = OWNERS // GROUP
 WIDE = GROUP * CAP
 EMPTY = 16777216.0
+STRAIGHT = 4
 
 
 def link_load(step):
@@ -89,7 +90,7 @@
     route = jnp.zeros((OWNERS, 128), jnp.int32)
     for index, step in enumerate(ORDER):
         route = jnp.where(slot == index, step[0] * 16 + step[1] * 4 + step[2], route)
-    digits = []
+    words = []
     for tile in range(8):
         ids = cluster[tile : tile + 1, :]
         owner = ids // 8
@@ -99,8 +100,7 @@
         code = step_y * 16 + step_z * 4 + step_x
         hit = jnp.where(route == code, 1.0, 0.0)
         hits[:, tile * 128 : (tile + 1) * 128] = hit.astype(jnp.bfloat16)
-        code = ids % 8 * RANKS + rank[tile : tile + 1, :] + 1
-        digits.append((code % 256, code // 256 % 256, code // 65536))
+        words.append(ids % 8 * RANKS + rank[tile : tile + 1, :] + 1)
     lower = lax.broadcasted_iota(jnp.int32, (256, 256), 0)
     upper = lax.broadcasted_iota(jnp.int32, (256, 256), 1)
     before = jnp.where(lower <= upper, 1.0, 0.0).astype(jnp.bfloat16)
@@ -110,12 +110,27 @@
         count = jnp.dot(hits[:, cols], before, preferred_element_type=jnp.float32) + carry
         carry = count[:, 255:256]
         place[:, cols] = jnp.where(hits[:, cols].astype(jnp.float32) > 0.5, count, 0.0)
-    digit = jnp.concatenate(
-        [jnp.concatenate([piece[row] for piece in digits], axis=1) for row in range(3)]
-        + [jnp.zeros((5, ROWS), jnp.int32)],
-        axis=0,
-    )
-    digit = digit.astype(jnp.float32).astype(jnp.bfloat16)
+    turn = lax.broadcasted_iota(jnp.int32, (OWNERS, ROWS), 0) % 4 * CAP
+    where = jnp.where(place[...] > 0.5, place[...] - 1.0 + turn.astype(jnp.float32), 0.0)
+    where = jnp.sum(where, axis=0, keepdims=True)
+    lane = lax.broadcasted_iota(jnp.int32, (128, ROWS), 0).astype(jnp.float32)
+    picks[...] = jnp.where(lane == where, 1.0, 0.0).astype(jnp.bfloat16)
+
+    word = jnp.concatenate(words, axis=1)
+    codes = jnp.zeros((OWNERS, 128), jnp.float32)
+    for power, digit in ((1, word % 256), (256, word // 256 % 256), (65536, word // 65536)):
+        marked = hits[...] * digit.astype(jnp.float32).astype(jnp.bfloat16)
+        codes = codes + nt_dot(marked, picks[...]) * float(power)
+    send_codes[...] = codes.reshape(OWNERS, 1, 128)
+    own_codes[0] = send_codes[0]
+    pl.semaphore_wait(barrier, OWNERS)
+    for index in range(1, OWNERS):
+        copy = pltpu.make_async_remote_copy(
+            src_ref=send_codes.at[index], dst_ref=own_codes.at[index],
+            send_sem=code_send, recv_sem=code_recv,
+            device_id=peer(ORDER[index], 1), device_id_type=MESH,
+        )
+        copy.start()
 
     loads[2].wait()
 
@@ -129,7 +144,6 @@
     lax.fori_loop(0, 8, normalise, 0)
 
     spot = lax.broadcasted_iota(jnp.int32, (CAP, ROWS), 0).astype(jnp.float32) + 1.0
-    row_copies, code_copies = [], []
     for group in range(GROUPS):
         for index in range(GROUP):
             line = place[group * GROUP + index : group * GROUP + index + 1, :]
@@ -138,23 +152,10 @@
         picked = jnp.dot(sel[...], unit[...], preferred_element_type=jnp.float32)
         picked = picked.astype(jnp.bfloat16).reshape(GROUP, CAP, D)
         send_rows[group * GROUP : (group + 1) * GROUP] = picked
-        parts = nt_dot(digit, sel[...])
-        codes = parts[0:1] + parts[1:2] * 256.0 + parts[2:3] * 65536.0
-        for index in range(GROUP):
-            half = index // 4 * 128
-            send_codes[group * GROUP + index] = codes[:, half : half + 128]
         if group == 0:
             own_rows[0] = picked[0]
-            own_codes[0] = codes[:, 0:128]
-            pl.semaphore_wait(barrier, OWNERS)
         for index in range(max(1, group * GROUP), (group + 1) * GROUP):
             target = peer(ORDER[index], 1)
-            copy = pltpu.make_async_remote_copy(
-                src_ref=send_codes.at[index], dst_ref=own_codes.at[index],
-                send_sem=code_send, recv_sem=code_recv,
-                device_id=target, device_id_type=MESH,
-            )
-            copy.start()
             copy = pltpu.make_async_remote_copy(
                 src_ref=send_rows.at[index], dst_ref=own_rows.at[index],
                 send_sem=row_send, recv_sem=row_recv.at[group],
@@ -162,17 +163,9 @@
             )
             copy.start()
 
-    turn = lax.broadcasted_iota(jnp.int32, (OWNERS, ROWS), 0) % 4 * CAP
-    where = jnp.where(place[...] > 0.5, place[...] - 1.0 + turn.astype(jnp.float32), 0.0)
-    where = jnp.sum(where, axis=0, keepdims=True)
-    lane = lax.broadcasted_iota(jnp.int32, (128, ROWS), 0).astype(jnp.float32)
-    picks[...] = jnp.where(lane == where, 1.0, 0.0).astype(jnp.bfloat16)
-
     def spread(codes, keys, is_own):
         block = codes[...].reshape(OWNERS // 4, 4, 1, 128)
-        part = lax.broadcasted_iota(jnp.int32, block.shape, 1)
-        at = lax.broadcasted_iota(jnp.int32, block.shape, 3) // CAP
-        line = jnp.sum(jnp.where(part == at, block, 0.0), axis=1)
+        line = jnp.sum(block, axis=1)
         if is_own:
             limits[0] = line
             limits[1] = jnp.floor((line - 1.0) * (1.0 / RANKS)) * float(RANKS) + 1.0
@@ -192,15 +185,19 @@
     best[...] = jnp.full(best.shape, -1.0, jnp.float32)
 
     def compare(query, blocks):
-        at = pl.multiple_of(query * GROUP, GROUP)
-        rows = own_rows[pl.ds(at, GROUP)].reshape(WIDE, D)
+        start = query * GROUP
+        if not isinstance(query, int):
+            start = pl.multiple_of(start, GROUP)
+        rows = own_rows[pl.ds(start, GROUP)].reshape(WIDE, D)
         high = limits[0, pl.ds(query * 2, 2)]
         low = limits[1, pl.ds(query * 2, 2)]
         tops = [best[query, :, half * 128 : (half + 1) * 128] for half in range(2)]
         for data, keys, block in blocks:
-            key_at = pl.multiple_of(block * GROUP, GROUP)
-            scores = nt_dot(data[pl.ds(key_at, GROUP)].reshape(WIDE, D), rows)
-            code = keys[pl.ds(pl.multiple_of(block * WIDE, WIDE), WIDE), :]
+            start, slots = block * GROUP, block * WIDE
+            if not isinstance(block, int):
+                start, slots = pl.multiple_of(start, GROUP), pl.multiple_of(slots, WIDE)
+            scores = nt_dot(data[pl.ds(start, GROUP)].reshape(WIDE, D), rows)
+            code = keys[pl.ds(slots, WIDE), :]
             for half in range(2):
                 allowed = (code < high[half]) & (code >= low[half])
                 part = scores[:, half * 128 : (half + 1) * 128]
@@ -210,57 +207,62 @@
             best[query, :, half * 128 : (half + 1) * 128] = tops[half]
 
     hops = []
-    for step in range(GROUPS + 1):
-        if step < GROUPS:
-            here = own_rows.at[max(1, step * GROUP) : (step + 1) * GROUP]
-            pltpu.make_async_copy(here, here, row_recv.at[step]).wait()
-            block = pl.ds(step * GROUP, GROUP)
-            hop = pltpu.make_async_remote_copy(
-                src_ref=own_rows.at[block], dst_ref=far_rows.at[block],
-                send_sem=far_send.at[step], recv_sem=far_recv.at[step],
-                device_id=sibling, device_id_type=MESH,
-            )
-            hop.start()
-            hops.append(hop)
-        fresh = []
-        if step < GROUPS:
-            fresh.append((own_rows, own_keys, step))
+    for step in range(GROUPS):
+        here = own_rows.at[max(1, step * GROUP) : (step + 1) * GROUP]
+        pltpu.make_async_copy(here, here, row_recv.at[step]).wait()
+        block = pl.ds(step * GROUP, GROUP)
+        hop = pltpu.make_async_remote_copy(
+            src_ref=own_rows.at[block], dst_ref=far_rows.at[block],
+            send_sem=far_send.at[step], recv_sem=far_recv.at[step],
+            device_id=sibling, device_id_type=MESH,
+        )
+        hop.start()
+        hops.append(hop)
+        own_block, far_block = (own_rows, own_keys, step), (far_rows, far_keys, step)
+        if step < STRAIGHT:
+
+            def earlier(block, _, step=step, own_block=own_block):
+                compare(block, [own_block])
+                compare(step, [(own_rows, own_keys, block), (far_rows, far_keys, block)])
+                return 0
+
+            lax.fori_loop(0, step, earlier, 0)
+            compare(step, [own_block])
+        else:
+            for query in range(step):
+                compare(query, [own_block])
+            before = [(own_rows, own_keys, block) for block in range(step + 1)]
+            before += [(far_rows, far_keys, block) for block in range(step)]
+            compare(step, before)
         if step == 0:
             code_hop.wait_recv()
             spread(far_codes, far_keys, False)
-        else:
-            hops[step - 1].wait_recv()
-            fresh.append((far_rows, far_keys, step - 1))
-
-        def old_queries(query, _, fresh=fresh):
-            compare(query, fresh)
-            return 0
-
-        if step < GROUPS:
-            lax.fori_loop(0, step, old_queries, 0)
-
-            def old_keys(block, _, step=step):
-                compare(step, [(own_rows, own_keys, block), (far_rows, far_keys, block)])
+        hop.wait_recv()
+        if step < STRAIGHT:
+
+            def others(query, _, far_block=far_block):
+                compare(query, [far_block])
                 return 0
 
-            lax.fori_loop(0, step, old_keys, 0)
-            compare(step, [(own_rows, own_keys, step)])
-        else:
-            for query in range(GROUPS):
-                compare(query, fresh)
-                for half in range(2):
-                    top = jnp.max(best[query, :, half * 128 : (half + 1) * 128], axis=0, keepdims=True)
-                    send_back[query * 2 + half] = top
-                for index in range(query * GROUP, (query + 1) * GROUP):
-                    if index == 0:
-                        got_back[0] = send_back[0]
-                        continue
-                    copy = pltpu.make_async_remote_copy(
-                        src_ref=send_back.at[index // 4], dst_ref=got_back.at[index],
-                        send_sem=back_send, recv_sem=back_recv,
-                        device_id=peer(ORDER[index], -1), device_id_type=MESH,
-                    )
-                    copy.start()
+            lax.fori_loop(0, step + 1, others, 0)
+            continue
+        for query in range(step + 1):
+            compare(query, [far_block])
+            if step < GROUPS - 1:
+                continue
+            for half in range(2):
+                top = jnp.max(best[query, :, half * 128 : (half + 1) * 128], axis=0, keepdims=True)
+                send_back[query * 2 + half] = top
+            for index in range(query * GROUP, (query + 1) * GROUP):
+                if index == 0:
+                    got_back[0] = send_back[0]
+                    continue
+                copy = pltpu.make_async_remote_copy(
+                    src_ref=send_back.at[index // 4], dst_ref=got_back.at[index],
+                    send_sem=back_send, recv_sem=back_recv,
+                    device_id=peer(ORDER[index], -1), device_id_type=MESH,
+                )
+                copy.start()
 
     pltpu.make_async_copy(got_back.at[1:], got_back.at[1:], back_recv).wait()
     back = got_back[...].reshape(OWNERS, 128)
@@ -327,7 +329,7 @@
             dma,
         ],
         compiler_params=pltpu.CompilerParams(
-            collective_id=0, has_side_effects=True, vmem_limit_bytes=40 * 2**20
+            collective_id=0, has_side_effects=True, vmem_limit_bytes=63 * 2**20
         ),
         cost_estimate=pl.CostEstimate(
             flops=2 * D * 2048 * (4096 + 1024), bytes_accessed=2 * ROWS * D, transcendentals=ROWS

time: 90.5 us -> 71.8 us (0.79)
  Pallas kernels: 86.8 us -> 70.4 us
  local copies, waits for them, and re-layouts: 3.38 us -> 1.28 us
    pallas_call x1, Pallas kernels: 86.8 us -> 70.4 us  [shards(): pl.pallas_call(kernel, out_shape=jax.ShapeDtypeStruct((8, 128), f32), in_...]
    unnamed x7 -> x1, local copies, waits for them, and re-layouts: 3.38 us -> 1.28 us
where the time goes in v2:
time: 71.8 us; the launch traced here: 71.7 us
  Pallas kernels  70.4 us (98%)
  local copies, waits for them, and re-layouts  1.28 us (2%)
    pallas_call x1, Pallas kernels, shards(): pl.pallas_call(kernel, out_shape=jax.ShapeDtypeStruct((8, 128), f32), in_...  70.4 us

profile of v2, /device:TPU:0, one launch (start us, length us, event | category | flops | bytes accessed | tf_op | source)
XLA Modules:
  0.0 71.7 jit_solution(138089354609073794)
XLA Ops:
  0.0 70.4 %dedup.1 = f32[8,128]{1,0:T(8,128)} custom-call(bf16[1024,768]{1,0:T(8,128)(2,1)} %emb_hbm.1, s32[8,128]{1,0:T(8,128)} %bitcast.4, s32[8,128]{1,0:T(8,128)} %bitcast.5), custom_call_target="tpu_custom_call" | custom-call | flops 16106127360 | bytes 1572864 | tf_op jit(solution)/shard_map/dedup/pallas_call | solution.py:295
  70.4 1.3 %copy.5 = f32[1024]{0:T(1024)} copy(f32[1024]{0:T(1024)} %bitcast.3) | data formatting | bytes 8192

commit v3 on v2

v3 whole, which is shorter than its diff:
```python
import functools

import jax
import jax.numpy as jnp
from jax import lax
from jax.experimental import pallas as pl
from jax.experimental.pallas import tpu as pltpu
from jax.sharding import PartitionSpec as P

MESH = pl.DeviceIdType.MESH
OWNERS = 64
CAP = 32
ROWS = 1024
D = 768
RANKS = 131072
GROUP = 8
GROUPS = OWNERS // GROUP
WIDE = GROUP * CAP
EMPTY = 16777216.0


PLAN = (
    (25, 5, 11, 96),
    (8, 48, 144, 13, 37),
    (111, 166, 91, 77, 83),
    (124, 140, 87, 183),
    (116, 60, 150, 16, 136),
    (108, 31, 161, 47),
    (163, 142, 53, 23, 69, 147),
    (92, 126, 76),
    (81, 165, 112, 184, 125, 131),
    (175, 152, 138),
    (17, 191, 114, 61, 46),
    (51, 162, 79, 32),
    (109, 88, 149, 143, 75, 159),
    (128, 123, 82),
    (90, 174, 22, 139, 113, 167),
    (130, 44, 135),
    (185, 71, 78, 189, 115, 187),
    (141, 172, 164),
    (160, 40, 89, 119, 66, 153),
    (176, 99, 127),
    (129, 19, 43, 137, 95),
    (178, 80, 63, 186),
    (173, 59, 72, 168, 70, 190),
    (117, 34, 68),
    (157, 85, 41, 155, 102),
    (20, 93, 180, 28),
    (54, 177, 64, 133, 188),
    (169, 101, 107, 120),
    (35, 57, 171, 73),
    (84, 156, 67, 104),
    (118, 94, 29),
    (65, 179, 132, 181),
    (105, 121, 56),
)
WAIT = 5
LAND = 4
CODES_AT = 2
CODES_LAND = 8
HOP = 2
PAIRS = 6
LAST_PAIRS = 32


def step_of(code):
    return (code // 16, code // 4 % 4, code % 4)


def travel():
    hops, done, order = [], {}, [0]
    for entries in PLAN:
        row = []
        for entry in entries:
            code, dim = entry // 3, entry % 3
            passed = done.setdefault(code, set())
            first = not passed
            passed.add(dim)
            last = passed == {axis for axis, part in enumerate(step_of(code)) if part}
            if last:
                order.append(code)
            row.append((code, dim, first, last))
        hops.append(row)
    return hops, order


HOPS, ARRIVALS = travel()
ORDER = [step_of(code) for code in ARRIVALS]
SLOT = {code: slot for slot, code in enumerate(ARRIVALS)}
TRANSITS = sum(not last for row in HOPS for _, _, _, last in row)


def nt_dot(a, b):
    return lax.dot_general(a, b, (((1,), (1,)), ((), ())), preferred_element_type=jnp.float32)


def kernel(
    emb_hbm, cluster_hbm, rank_hbm, out_ref,
    emb, cluster, rank, unit, hits, place, sel, picks,
    send_rows, transit, own_rows, far_rows, send_codes, own_codes, far_codes,
    own_keys, far_keys, limits, best, send_back, got_back,
    load_sem, row_send, pass_send, pass_recv, row_recv, code_send, code_recv, far_send, far_recv, back_send, back_recv,
):
    me = lax.axis_index("dp")
    core = lax.axis_index("split")
    my, mz, mx = me // 16, me // 4 % 4, me % 4

    def peer(step, sign):
        y = (my + sign * step[0] + 4) % 4
        z = (mz + sign * step[1] + 4) % 4
        x = (mx + sign * step[2] + 4) % 4
        return (y * 16 + z * 4 + x, core)

    sibling = (me, 1 - core)

    loads = [
        pltpu.make_async_copy(source, target, load_sem.at[index])
        for index, (source, target) in enumerate(
            ((cluster_hbm, cluster), (rank_hbm, rank), (emb_hbm, emb))
        )
    ]
    for load in loads:
        load.start()
    barrier = pltpu.get_barrier_semaphore()
    for step in ORDER[1:]:
        pl.semaphore_signal(barrier, inc=1, device_id=peer(step, 1), device_id_type=MESH)
    pl.semaphore_signal(barrier, inc=1, device_id=sibling, device_id_type=MESH)

    loads[0].wait()
    loads[1].wait()
    slot = lax.broadcasted_iota(jnp.int32, (OWNERS, 128), 0)
    route = jnp.zeros((OWNERS, 128), jnp.int32)
    for index, step in enumerate(ORDER):
        route = jnp.where(slot == index, step[0] * 16 + step[1] * 4 + step[2], route)
    words = []
    for tile in range(8):
        ids = cluster[tile : tile + 1, :]
        owner = ids // 8
        step_y = (owner // 16 - my + 4) % 4
        step_z = (owner // 4 % 4 - mz + 4) % 4
        step_x = (owner % 4 - mx + 4) % 4
        code = step_y * 16 + step_z * 4 + step_x
        hit = jnp.where(route == code, 1.0, 0.0)
        hits[:, tile * 128 : (tile + 1) * 128] = hit.astype(jnp.bfloat16)
        words.append(ids % 8 * RANKS + rank[tile : tile + 1, :] + 1)
    lower = lax.broadcasted_iota(jnp.int32, (256, 256), 0)
    upper = lax.broadcasted_iota(jnp.int32, (256, 256), 1)
    before = jnp.where(lower <= upper, 1.0, 0.0).astype(jnp.bfloat16)
    carry = jnp.zeros((OWNERS, 1), jnp.float32)
    for part in range(4):
        cols = slice(part * 256, (part + 1) * 256)
        count = jnp.dot(hits[:, cols], before, preferred_element_type=jnp.float32) + carry
        carry = count[:, 255:256]
        place[:, cols] = jnp.where(hits[:, cols].astype(jnp.float32) > 0.5, count, 0.0)
    loads[2].wait()

    def normalise(index, _):
        rows = pl.ds(pl.multiple_of(index * 128, 128), 128)
        values = emb[rows, :].astype(jnp.float32)
        total = jnp.sum(values * values, axis=1, keepdims=True)
        unit[rows, :] = (values * lax.rsqrt(total + 1e-06)).astype(jnp.bfloat16)
        return 0

    lax.fori_loop(0, 8, normalise, 0)

    leaving = [SLOT[code] for row in HOPS for code, _, first, _ in row if first]
    leaving.insert(GROUP * 2 - 1, 0)
    spot = lax.broadcasted_iota(jnp.int32, (CAP, ROWS), 0).astype(jnp.float32) + 1.0
    selected = []

    def select_until(count):
        while len(selected) < count:
            slots = leaving[len(selected) : len(selected) + GROUP]
            for index, slot in enumerate(slots):
                line = place[slot : slot + 1, :]
                chosen = jnp.where(jnp.broadcast_to(line, (CAP, ROWS)) == spot, 1.0, 0.0)
                sel[index * CAP : (index + 1) * CAP, :] = chosen.astype(jnp.bfloat16)
            picked = jnp.dot(sel[...], unit[...], preferred_element_type=jnp.float32)
            picked = picked.astype(jnp.bfloat16).reshape(GROUP, CAP, D)
            for index, slot in enumerate(slots):
                if slot == 0:
                    own_rows[0] = picked[index]
                else:
                    send_rows[slot] = picked[index]
            selected.extend(slots)

    def needed(number):
        slots = [SLOT[code] for row in HOPS[: number + 1] for code, _, first, _ in row if first]
        return max((leaving.index(slot) + 1 for slot in slots), default=0)

    def send_all_codes():
        turn = lax.broadcasted_iota(jnp.int32, (OWNERS, ROWS), 0) % 4 * CAP
        where = jnp.where(place[...] > 0.5, place[...] - 1.0 + turn.astype(jnp.float32), 0.0)
        where = jnp.sum(where, axis=0, keepdims=True)
        lane = lax.broadcasted_iota(jnp.int32, (128, ROWS), 0).astype(jnp.float32)
        picks[...] = jnp.where(lane == where, 1.0, 0.0).astype(jnp.bfloat16)

        word = jnp.concatenate(words, axis=1)
        codes = jnp.zeros((OWNERS, 128), jnp.float32)
        for power, digit in ((1, word % 256), (256, word // 256 % 256), (65536, word // 65536)):
            marked = hits[...] * digit.astype(jnp.float32).astype(jnp.bfloat16)
            codes = codes + nt_dot(marked, picks[...]) * float(power)
        send_codes[...] = codes.reshape(OWNERS, 1, 128)
        own_codes[0] = send_codes[0]
        for index in range(1, OWNERS):
            copy = pltpu.make_async_remote_copy(
                src_ref=send_codes.at[index], dst_ref=own_codes.at[index],
                send_sem=code_send, recv_sem=code_recv,
                device_id=peer(ORDER[index], 1), device_id_type=MESH,
            )
            copy.start()

    def spread(codes, keys, is_own):
        block = codes[...].reshape(OWNERS // 4, 4, 1, 128)
        line = jnp.sum(block, axis=1)
        if is_own:
            limits[0] = line
            limits[1] = jnp.floor((line - 1.0) * (1.0 / RANKS)) * float(RANKS) + 1.0
        line = jnp.where(line == 0.0, EMPTY, line)
        for index in range(OWNERS // 4):
            square = jnp.broadcast_to(line[index], (128, 128))
            keys[index * 128 : (index + 1) * 128, :] = square.T

    def compare(query, blocks):
        rows = own_rows[query * GROUP : (query + 1) * GROUP].reshape(WIDE, D)
        high = limits[0, query * 2 : query * 2 + 2]
        low = limits[1, query * 2 : query * 2 + 2]
        tops = [best[query, :, half * 128 : (half + 1) * 128] for half in range(2)]
        for is_far, block in blocks:
            data, keys = (far_rows, far_keys) if is_far else (own_rows, own_keys)
            scores = nt_dot(data[block * GROUP : (block + 1) * GROUP].reshape(WIDE, D), rows)
            code = keys[block * WIDE : (block + 1) * WIDE, :]
            for half in range(2):
                allowed = (code < high[half]) & (code >= low[half])
                part = scores[:, half * 128 : (half + 1) * 128]
                part = jnp.where(allowed, part, -1.0).reshape(WIDE // 8, 8, 128)
                tops[half] = jnp.maximum(tops[half], jnp.max(part, axis=0))
        for half in range(2):
            best[query, :, half * 128 : (half + 1) * 128] = tops[half]

    def finish():
        tops = jnp.max(best[...], axis=1)
        for query in range(GROUPS):
            for half in range(2):
                send_back[query * 2 + half] = tops[query : query + 1, half * 128 : (half + 1) * 128]
        got_back[0] = send_back[0]
        for index in range(1, OWNERS):
            copy = pltpu.make_async_remote_copy(
                src_ref=send_back.at[index // 4], dst_ref=got_back.at[index],
                send_sem=back_send, recv_sem=back_recv,
                device_id=peer(ORDER[index], -1), device_id_type=MESH,
            )
            copy.start()

    best[...] = jnp.full(best.shape, -1.0, jnp.float32)
    queries, blocks, pairs, hops = [], [], [], []

    def compare_some(count):
        now = pairs[:count]
        del pairs[:count]
        while now:
            query = now[0][0]
            together = [block for other, block in now if other == query]
            now = [pair for pair in now if pair[0] != query]
            compare(query, together)

    def exchange(source, target, index):
        hop = pltpu.make_async_remote_copy(
            src_ref=source, dst_ref=target,
            send_sem=far_send.at[index], recv_sem=far_recv.at[index],
            device_id=sibling, device_id_type=MESH,
        )
        hop.start()
        hops.append(hop)
        return hop

    def codes_here():
        pltpu.make_async_copy(own_codes.at[1:], own_codes.at[1:], code_recv).wait()
        hop = exchange(own_codes, far_codes, GROUPS)
        spread(own_codes, own_keys, True)
        return lambda: codes_there(hop)

    def codes_there(hop):
        hop.wait_recv()
        spread(far_codes, far_keys, False)

    def group_here(group):
        here = own_rows.at[max(1, group * GROUP) : (group + 1) * GROUP]
        pltpu.make_async_copy(here, here, row_recv.at[group]).wait()
        rows = pl.ds(group * GROUP, GROUP)
        hop = exchange(own_rows.at[rows], far_rows.at[rows], group)
        pairs.extend((query, (False, group)) for query in queries)
        queries.append(group)
        blocks.append((False, group))
        pairs.extend((group, block) for block in blocks)
        return lambda: group_there(group, hop)

    def group_there(group, hop):
        hop.wait_recv()
        if group == GROUPS - 1:
            compare_some(len(pairs))
            for query in queries:
                compare(query, [(True, group)])
            finish()
            return
        blocks.append((True, group))
        pairs.extend((query, (True, group)) for query in queries)

    events, arrived = {}, 0
    for number, row in enumerate(HOPS):
        arrived += sum(last for _, _, _, last in row)
        for group in range(GROUPS):
            if arrived >= group * GROUP + GROUP - 1 and group not in events:
                events[group] = number + LAND
    todo = [(CODES_LAND, codes_here)]
    todo += [(max(CODES_LAND, events[group]), functools.partial(group_here, group)) for group in range(GROUPS)]
    parked, pass_at, number = {}, 0, 0
    select_until(needed(CODES_AT - 1))
    pl.semaphore_wait(barrier, OWNERS)
    while number < len(HOPS) or todo or pairs:
        if number == CODES_AT:
            send_all_codes()
        if number < len(HOPS):
            if number >= WAIT and number - WAIT in parked:
                here = transit.at[parked[number - WAIT]]
                pltpu.make_async_copy(here, here, pass_recv.at[number - WAIT]).wait()
            start = pass_at
            for code, dim, first, last in HOPS[number]:
                slot = SLOT[code]
                target = [0, 0, 0]
                target[dim] = step_of(code)[dim]
                if last:
                    place_there, arrival = own_rows.at[slot], row_recv.at[slot // GROUP]
                else:
                    place_there, arrival = transit.at[pass_at], pass_recv.at[number]
                copy = pltpu.make_async_remote_copy(
                    src_ref=send_rows.at[slot] if first else transit.at[parked[code, "at"]],
                    dst_ref=place_there,
                    send_sem=row_send if first else pass_send,
                    recv_sem=arrival,
                    device_id=peer(target, 1), device_id_type=MESH,
                )
                copy.start()
                if not last:
                    parked[code, "at"] = pass_at
                    pass_at += 1
            if pass_at > start:
                parked[number] = pl.ds(start, pass_at - start)
            select_until(needed(number + 2))
        for event in [event for event in todo if event[0] <= number]:
            todo.remove(event)
            following = event[1]()
            if following:
                todo.append((number + HOP, following))
        compare_some(PAIRS if number < len(HOPS) else LAST_PAIRS)
        number += 1

    pltpu.make_async_copy(got_back.at[1:], got_back.at[1:], back_recv).wait()
    back = got_back[...].reshape(OWNERS, 128)
    first = back.astype(jnp.bfloat16)
    rest = back - first.astype(jnp.float32)
    second = rest.astype(jnp.bfloat16)
    third = (rest - second.astype(jnp.float32)).astype(jnp.bfloat16)
    moved = [
        jnp.dot(piece, picks[...], preferred_element_type=jnp.float32)
        for piece in (first, second, third)
    ]
    moved = moved[0] + moved[1] + moved[2]
    result = jnp.sum(jnp.where(place[...] > 0.5, moved, 0.0), axis=0, keepdims=True)
    for tile in range(8):
        out_ref[tile : tile + 1, :] = result[:, tile * 128 : (tile + 1) * 128]

    pltpu.make_async_copy(send_rows.at[1:], send_rows.at[1:], row_send).wait()
    pltpu.make_async_copy(transit, transit, pass_send).wait()
    pltpu.make_async_copy(send_codes.at[1:], send_codes.at[1:], code_send).wait()
    pltpu.make_async_copy(got_back.at[1:], got_back.at[1:], back_send).wait()
    for hop in hops:
        hop.wait_send()


def shards(embeddings, cluster, rank):
    rows = (OWNERS, CAP, D)
    codes = (OWNERS, 1, 128)
    f32, bf16 = jnp.float32, jnp.bfloat16
    dma = pltpu.SemaphoreType.DMA
    result = pl.pallas_call(
        kernel,
        out_shape=jax.ShapeDtypeStruct((8, 128), f32),
        in_specs=[pl.BlockSpec(memory_space=pltpu.HBM)] * 3,
        out_specs=pl.BlockSpec(memory_space=pltpu.VMEM),
        scratch_shapes=[
            pltpu.VMEM((ROWS, D), bf16),
            pltpu.VMEM((8, 128), jnp.int32),
            pltpu.VMEM((8, 128), jnp.int32),
            pltpu.VMEM((ROWS, D), bf16),
            pltpu.VMEM((OWNERS, ROWS), bf16),
            pltpu.VMEM((OWNERS, ROWS), f32),
            pltpu.VMEM((WIDE, ROWS), bf16),
            pltpu.VMEM((128, ROWS), bf16),
            pltpu.VMEM(rows, bf16),
            pltpu.VMEM((TRANSITS, CAP, D), bf16),
            pltpu.VMEM(rows, bf16),
            pltpu.VMEM(rows, bf16),
            pltpu.VMEM(codes, f32),
            pltpu.VMEM(codes, f32),
            pltpu.VMEM(codes, f32),
            pltpu.VMEM((OWNERS * CAP, 128), f32),
            pltpu.VMEM((OWNERS * CAP, 128), f32),
            pltpu.VMEM((2, OWNERS // 4, 1, 128), f32),
            pltpu.VMEM((GROUPS, 8, WIDE), f32),
            pltpu.VMEM((OWNERS // 4, 1, 128), f32),
            pltpu.VMEM(codes, f32),
            dma((3,)),
            dma,
            dma,
            dma((len(HOPS),)),
            dma((GROUPS,)),
            dma,
            dma,
            dma((GROUPS + 1,)),
            dma((GROUPS + 1,)),
            dma,
            dma,
        ],
        compiler_params=pltpu.CompilerParams(
            collective_id=0, has_side_effects=True, vmem_limit_bytes=63 * 2**20
        ),
        cost_estimate=pl.CostEstimate(
            flops=2 * D * 2048 * (4096 + 1024), bytes_accessed=2 * ROWS * D, transcendentals=ROWS
        ),
        name="dedup",
    )(embeddings, cluster.reshape(8, 128), rank.reshape(8, 128))
    return result.reshape(ROWS)


def solution(mesh):
    in_specs = (P(("dp", "split"), None), P(("dp", "split")), P(("dp", "split")))
    out_specs = P(("dp", "split"))
    return jax.shard_map(shards, mesh=mesh, in_specs=in_specs, out_specs=out_specs, check_vma=False)
```

time: 71.8 us -> 64.1 us (0.89)
  Pallas kernels: 70.4 us -> 62.7 us
    pallas_call x1, Pallas kernels: 70.4 us -> 62.7 us  [shards(): pl.pallas_call(kernel, out_shape=jax.ShapeDtypeStruct((8, 128), f32), in_...]
where the time goes in v3:
time: 64.1 us; the launch traced here: 64 us
  Pallas kernels  62.7 us (98%)
  local copies, waits for them, and re-layouts  1.28 us (2%)
    pallas_call x1, Pallas kernels, shards(): pl.pallas_call(kernel, out_shape=jax.ShapeDtypeStruct((8, 128), f32), in_...  62.7 us

profile of v3, /device:TPU:0, one launch (start us, length us, event | category | flops | bytes accessed | tf_op | source)
XLA Modules:
  0.0 64.0 jit_solution(15139252412653220865)
XLA Ops:
  0.0 62.7 %dedup.1 = f32[8,128]{1,0:T(8,128)} custom-call(bf16[1024,768]{1,0:T(8,128)(2,1)} %emb_hbm.1, s32[8,128]{1,0:T(8,128)} %bitcast.4, s32[8,128]{1,0:T(8,128)} %bitcast.5), custom_call_target="tpu_custom_call" | custom-call | flops 16106127360 | bytes 1572864 | tf_op jit(solution)/shard_map/dedup/pallas_call | solution.py:386
  62.7 1.3 %copy.5 = f32[1024]{0:T(1024)} copy(f32[1024]{0:T(1024)} %bitcast.3) | data formatting | bytes 8192

commit v4 on v3

--- a/solution.py
+++ b/solution.py
@@ -55,16 +55,20 @@
     (105, 121, 56),
 )
 WAIT = 5
-LAND = 4
+LAND = 5
 CODES_AT = 2
 CODES_LAND = 8
 HOP = 2
-PAIRS = 6
+PAIRS = 7
 LAST_PAIRS = 32
 
 
 def step_of(code):
     return (code // 16, code // 4 % 4, code % 4)
+
+
+def hops_of(step):
+    return sum(min(part, 4 - part) for part in step)
 
 
 def travel():
@@ -244,7 +248,7 @@
             for half in range(2):
                 send_back[query * 2 + half] = tops[query : query + 1, half * 128 : (half + 1) * 128]
         got_back[0] = send_back[0]
-        for index in range(1, OWNERS):
+        for index in sorted(range(1, OWNERS), key=lambda index: -hops_of(ORDER[index])):
             copy = pltpu.make_async_remote_copy(
                 src_ref=send_back.at[index // 4], dst_ref=got_back.at[index],
                 send_sem=back_send, recv_sem=back_recv,
@@ -361,11 +365,10 @@
     rest = back - first.astype(jnp.float32)
     second = rest.astype(jnp.bfloat16)
     third = (rest - second.astype(jnp.float32)).astype(jnp.bfloat16)
-    moved = [
-        jnp.dot(piece, picks[...], preferred_element_type=jnp.float32)
-        for piece in (first, second, third)
-    ]
-    moved = moved[0] + moved[1] + moved[2]
+    moved = jnp.dot(
+        jnp.concatenate([first, second, third], axis=0), picks[...], preferred_element_type=jnp.float32
+    )
+    moved = moved[:OWNERS] + moved[OWNERS : 2 * OWNERS] + moved[2 * OWNERS :]
     result = jnp.sum(jnp.where(place[...] > 0.5, moved, 0.0), axis=0, keepdims=True)
     for tile in range(8):
         out_ref[tile : tile + 1, :] = result[:, tile * 128 : (tile + 1) * 128]
@@ -382,6 +385,7 @@
     rows = (OWNERS, CAP, D)
     codes = (OWNERS, 1, 128)
     f32, bf16 = jnp.float32, jnp.bfloat16
+    operands = (embeddings, cluster.reshape(8, 128), rank.reshape(8, 128))
     dma = pltpu.SemaphoreType.DMA
     result = pl.pallas_call(
         kernel,
@@ -423,13 +427,13 @@
             dma,
         ],
         compiler_params=pltpu.CompilerParams(
-            collective_id=0, has_side_effects=True, vmem_limit_bytes=63 * 2**20
+            collective_id=0, has_side_effects=True, vmem_limit_bytes=48 * 2**20
         ),
         cost_estimate=pl.CostEstimate(
             flops=2 * D * 2048 * (4096 + 1024), bytes_accessed=2 * ROWS * D, transcendentals=ROWS
         ),
         name="dedup",
-    )(embeddings, cluster.reshape(8, 128), rank.reshape(8, 128))
+    )(*(pltpu.with_memory_space_constraint(operand, pltpu.HBM) for operand in operands))
     return result.reshape(ROWS)
 
 

time: 64.1 us -> 61.5 us (0.959)
  Pallas kernels: 62.7 us -> 60.8 us
  local copies, waits for them, and re-layouts: 1.28 us -> 0.6 us
    pallas_call x1, Pallas kernels: 62.7 us -> 60.8 us  [shards(): pl.pallas_call(kernel, out_shape=jax.ShapeDtypeStruct((8, 128), f32), in_...]
    unnamed x1, local copies, waits for them, and re-layouts: 1.28 us -> 0.6 us
where the time goes in v4:
time: 61.5 us; the launch traced here: 61.4 us
  Pallas kernels  60.8 us (99%)
    pallas_call x1, Pallas kernels, shards(): pl.pallas_call(kernel, out_shape=jax.ShapeDtypeStruct((8, 128), f32), in_...  60.8 us

profile of v4, /device:TPU:0, one launch (start us, length us, event | category | flops | bytes accessed | tf_op | source)
XLA Modules:
  0.0 61.4 jit_solution(8968968337211728421)
XLA Ops:
  0.0 60.8 %dedup.1 = f32[8,128]{1,0:T(8,128)S(1)} custom-call(bf16[1024,768]{1,0:T(8,128)(2,1)} %emb_hbm.1, s32[8,128]{1,0:T(8,128)} %bitcast.4, s32[8,128]{1,0:T(8,128)} %bitcast.5), custom_call_target="tpu_custom_call" | custom-call | flops 16106127360 | bytes 1572864 | tf_op jit(solution)/shard_map/dedup/pallas_call | solution.py:390
  60.8 0.6 copy.5

commit v5 on v4

--- a/solution.py
+++ b/solution.py
@@ -56,8 +56,9 @@
 )
 WAIT = 5
 LAND = 5
-CODES_AT = 2
-CODES_LAND = 8
+PLANE_AT = 2
+CODES_AT = 4
+CODES_LAND = 9
 HOP = 2
 PAIRS = 7
 LAST_PAIRS = 32
@@ -104,6 +105,7 @@
     send_rows, transit, own_rows, far_rows, send_codes, own_codes, far_codes,
     own_keys, far_keys, limits, best, send_back, got_back,
     load_sem, row_send, pass_send, pass_recv, row_recv, code_send, code_recv, far_send, far_recv, back_send, back_recv,
+    plane_sem, cube_sem,
 ):
     me = lax.axis_index("dp")
     core = lax.axis_index("split")
@@ -116,6 +118,10 @@
         return (y * 16 + z * 4 + x, core)
 
     sibling = (me, 1 - core)
+
+    def line(dim):
+        return [peer([part if axis == dim else 0 for axis in range(3)], 1) for part in (1, 2, 3)]
+
 
     loads = [
         pltpu.make_async_copy(source, target, load_sem.at[index])
@@ -126,9 +132,14 @@
     for load in loads:
         load.start()
     barrier = pltpu.get_barrier_semaphore()
-    for step in ORDER[1:]:
-        pl.semaphore_signal(barrier, inc=1, device_id=peer(step, 1), device_id_type=MESH)
+    for dim in range(3):
+        for target in line(dim):
+            pl.semaphore_signal(barrier, inc=1, device_id=target, device_id_type=MESH)
     pl.semaphore_signal(barrier, inc=1, device_id=sibling, device_id_type=MESH)
+
+    def greet(sem, dim):
+        for target in line(dim):
+            pl.semaphore_signal(sem, inc=1, device_id=target, device_id_type=MESH)
 
     loads[0].wait()
     loads[1].wait()
@@ -158,14 +169,10 @@
         place[:, cols] = jnp.where(hits[:, cols].astype(jnp.float32) > 0.5, count, 0.0)
     loads[2].wait()
 
-    def normalise(index, _):
-        rows = pl.ds(pl.multiple_of(index * 128, 128), 128)
-        values = emb[rows, :].astype(jnp.float32)
+    for start in range(0, ROWS, 128):
+        values = emb[start : start + 128, :].astype(jnp.float32)
         total = jnp.sum(values * values, axis=1, keepdims=True)
-        unit[rows, :] = (values * lax.rsqrt(total + 1e-06)).astype(jnp.bfloat16)
-        return 0
-
-    lax.fori_loop(0, 8, normalise, 0)
+        unit[start : start + 128, :] = (values * lax.rsqrt(total + 1e-06)).astype(jnp.bfloat16)
 
     leaving = [SLOT[code] for row in HOPS for code, _, first, _ in row if first]
     leaving.insert(GROUP * 2 - 1, 0)
@@ -320,9 +327,14 @@
     todo += [(max(CODES_LAND, events[group]), functools.partial(group_here, group)) for group in range(GROUPS)]
     parked, pass_at, number = {}, 0, 0
     select_until(needed(CODES_AT - 1))
-    pl.semaphore_wait(barrier, OWNERS)
+    pl.semaphore_wait(barrier, 10)
+    greet(plane_sem, 2)
     while number < len(HOPS) or todo or pairs:
+        if number == PLANE_AT:
+            pl.semaphore_wait(plane_sem, 3)
+            greet(cube_sem, 1)
         if number == CODES_AT:
+            pl.semaphore_wait(cube_sem, 3)
             send_all_codes()
         if number < len(HOPS):
             if number >= WAIT and number - WAIT in parked:
@@ -425,6 +437,8 @@
             dma((GROUPS + 1,)),
             dma,
             dma,
+            pltpu.SemaphoreType.REGULAR,
+            pltpu.SemaphoreType.REGULAR,
         ],
         compiler_params=pltpu.CompilerParams(
             collective_id=0, has_side_effects=True, vmem_limit_bytes=48 * 2**20

time: 61.5 us -> 60.4 us (0.982)
  Pallas kernels: 60.8 us -> 59.6 us
    pallas_call x1, Pallas kernels: 60.8 us -> 59.6 us  [shards(): pl.pallas_call(kernel, out_shape=jax.ShapeDtypeStruct((8, 128), f32), in_...]
where the time goes in v5:
time: 60.4 us; the launch traced here: 60.2 us
  Pallas kernels  59.6 us (99%)
    pallas_call x1, Pallas kernels, shards(): pl.pallas_call(kernel, out_shape=jax.ShapeDtypeStruct((8, 128), f32), in_...  59.6 us

profile of v5, /device:TPU:0, one launch (start us, length us, event | category | flops | bytes accessed | tf_op | source)
XLA Modules:
  0.0 60.2 jit_solution(7073375601686714104)
XLA Ops:
  0.0 59.6 %dedup.1 = f32[8,128]{1,0:T(8,128)S(1)} custom-call(bf16[1024,768]{1,0:T(8,128)(2,1)} %emb_hbm.1, s32[8,128]{1,0:T(8,128)} %bitcast.4, s32[8,128]{1,0:T(8,128)} %bitcast.5), custom_call_target="tpu_custom_call" | custom-call | flops 16106127360 | bytes 1572864 | tf_op jit(solution)/shard_map/dedup/pallas_call | solution.py:402
  59.6 0.6 copy.5

commit v6 on v5

--- a/solution.py
+++ b/solution.py
@@ -60,6 +60,7 @@
 CODES_AT = 4
 CODES_LAND = 9
 HOP = 2
+BOTH_FROM = 4
 PAIRS = 7
 LAST_PAIRS = 32
 
@@ -232,6 +233,19 @@
             square = jnp.broadcast_to(line[index], (128, 128))
             keys[index * 128 : (index + 1) * 128, :] = square.T
 
+    def compare_back(scores, code, high, block):
+        base = jnp.floor((code - 1.0) * (1.0 / RANKS)) * float(RANKS) + 1.0
+        top = None
+        for half in range(2):
+            key = jnp.where(high[half] == 0.0, EMPTY, high[half])
+            part = scores[:, half * 128 : (half + 1) * 128]
+            part = jnp.where((key < code) & (key >= base), part, -1.0)
+            top = part if top is None else jnp.maximum(top, part)
+        for half in range(2):
+            cols = slice(half * 128, (half + 1) * 128)
+            line = jnp.max(top[cols, :].T, axis=0, keepdims=True)
+            best[block, 0:1, cols] = jnp.maximum(best[block, 0:1, cols], line)
+
     def compare(query, blocks):
         rows = own_rows[query * GROUP : (query + 1) * GROUP].reshape(WIDE, D)
         high = limits[0, query * 2 : query * 2 + 2]
@@ -246,6 +260,8 @@
                 part = scores[:, half * 128 : (half + 1) * 128]
                 part = jnp.where(allowed, part, -1.0).reshape(WIDE // 8, 8, 128)
                 tops[half] = jnp.maximum(tops[half], jnp.max(part, axis=0))
+            if is_far is None:
+                compare_back(scores, code, high, block)
         for half in range(2):
             best[query, :, half * 128 : (half + 1) * 128] = tops[half]
 
@@ -300,10 +316,13 @@
         pltpu.make_async_copy(here, here, row_recv.at[group]).wait()
         rows = pl.ds(group * GROUP, GROUP)
         hop = exchange(own_rows.at[rows], far_rows.at[rows], group)
-        pairs.extend((query, (False, group)) for query in queries)
+        if group < BOTH_FROM:
+            pairs.extend((query, (False, group)) for query in queries)
         queries.append(group)
         blocks.append((False, group))
-        pairs.extend((group, block) for block in blocks)
+        for is_far, block in blocks:
+            both = group >= BOTH_FROM and not is_far and block != group
+            pairs.append((group, (None if both else is_far, block)))
         return lambda: group_there(group, hop)
 
     def group_there(group, hop):
@@ -367,7 +386,7 @@
             todo.remove(event)
             following = event[1]()
             if following:
-                todo.append((number + HOP, following))
+                todo.append((number + (HOP if number < len(HOPS) else 1), following))
         compare_some(PAIRS if number < len(HOPS) else LAST_PAIRS)
         number += 1
 

time: 60.4 us -> 59.8 us (0.990)
  no operation moved by 1% of the time
where the time goes in v6:
time: 59.8 us; the launch traced here: 59.6 us
  Pallas kernels  59 us (99%)
  local copies, waits for them, and re-layouts  0.6 us (1%)
    pallas_call x1, Pallas kernels, shards(): pl.pallas_call(kernel, out_shape=jax.ShapeDtypeStruct((8, 128), f32), in_...  59 us

profile of v6, /device:TPU:0, one launch (start us, length us, event | category | flops | bytes accessed | tf_op | source)
XLA Modules:
  0.0 59.6 jit_solution(17388964132992341756)
XLA Ops:
  0.0 59.0 %dedup.1 = f32[8,128]{1,0:T(8,128)S(1)} custom-call(bf16[1024,768]{1,0:T(8,128)(2,1)} %emb_hbm.1, s32[8,128]{1,0:T(8,128)} %bitcast.4, s32[8,128]{1,0:T(8,128)} %bitcast.5), custom_call_target="tpu_custom_call" | custom-call | flops 16106127360 | bytes 1572864 | tf_op jit(solution)/shard_map/dedup/pallas_call | solution.py:421
  59.1 0.6 copy.5

commit v7 on v6

--- a/solution.py
+++ b/solution.py
@@ -386,7 +386,7 @@
             todo.remove(event)
             following = event[1]()
             if following:
-                todo.append((number + (HOP if number < len(HOPS) else 1), following))
+                todo.append((number + HOP, following))
         compare_some(PAIRS if number < len(HOPS) else LAST_PAIRS)
         number += 1
 

time: 59.8 us -> 59.4 us (level)
  no operation moved by 1% of the time
where the time goes in v7:
time: 59.4 us; the launch traced here: 59.2 us
  Pallas kernels  58.6 us (99%)
  local copies, waits for them, and re-layouts  0.6 us (1%)
    pallas_call x1, Pallas kernels, shards(): pl.pallas_call(kernel, out_shape=jax.ShapeDtypeStruct((8, 128), f32), in_...  58.6 us

profile of v7, /device:TPU:0, one launch (start us, length us, event | category | flops | bytes accessed | tf_op | source)
XLA Modules:
  0.0 59.2 jit_solution(13678853556420078945)
XLA Ops:
  0.0 58.6 %dedup.1 = f32[8,128]{1,0:T(8,128)S(1)} custom-call(bf16[1024,768]{1,0:T(8,128)(2,1)} %emb_hbm.1, s32[8,128]{1,0:T(8,128)} %bitcast.4, s32[8,128]{1,0:T(8,128)} %bitcast.5), custom_call_target="tpu_custom_call" | custom-call | flops 16106127360 | bytes 1572864 | tf_op jit(solution)/shard_map/dedup/pallas_call | solution.py:421
  58.6 0.6 %copy.5 = f32[1024]{0:T(1024)} copy(f32[1024]{0:T(1024)S(1)} %bitcast.3) | data formatting | bytes 8192
